TPU v7x, 32 devices: a whole 2x2x4 slice. The times are simulated.
32 devices in a mesh: rep: 8 (over y, x, core), shard: 4 (over z).
Axes of the slice: x: 2, y: 2, z: 4, core: 2. Of those that a mesh axis runs over, the one named last changes fastest.
Arguments:
- grads_matrix: bfloat16 [8, 4, 3, 1024, 1024], P('rep', 'shard'), may hold values from -400 to 400
- grads_vector: bfloat16 [8, 4, 5, 1024], P('rep', 'shard'), may hold values from -6 to 6
- master_matrix: float32 [3, 1024, 1024], P(None, 'shard'), may hold values from -0.1875 to 0.1875
- master_vector: float32 [5, 1024], P(None, 'shard'), may hold values from 0.5 to 1.5
- moment_matrix: float32 [3, 1024, 1024], P(None, 'shard'), may hold values from -4 to 4
- moment_vector: float32 [5, 1024], P(None, 'shard'), may hold values from -4 to 4
- second_matrix: float32 [3, 1024, 1024], P(None, 'shard'), may hold values from 0.05 to 2
- second_vector: float32 [5, 1024], P(None, 'shard'), may hold values from 0.05 to 2
Outputs:
- matrix_master: float32 [3, 1024, 1024], P(None, 'shard')
- vector_master: float32 [5, 1024], P(None, 'shard')
- matrix_moment: float32 [3, 1024, 1024], P(None, 'shard')
- vector_moment: float32 [5, 1024], P(None, 'shard')
- matrix_second: float32 [3, 1024, 1024], P(None, 'shard')
- vector_second: float32 [5, 1024], P(None, 'shard')
- matrix_weights: bfloat16 [3, 1024, 1024], replicated
- vector_weights: bfloat16 [5, 1024], replicated
All inputs are finite; a program needn't handle non-finite values.
Results may differ from a plain program's by a relative error of at most 0.005.
Values may be sent and summed in bfloat16 or wider, within the bound.
A program may use at most 128 MiB of HBM per device.

v0:
```python
import jax
import jax.numpy as jnp
from jax import lax
from jax.sharding import PartitionSpec as P

STEP = 1000


beta_first = 0.9
beta_second = 0.999
learn_rate = 0.01
decay_rate = 0.1
epsilon = 1e-08


def adam_piece(total, master, moment, second, clip, decay):
    scaled = total * clip
    moment_next = beta_first * moment + (1.0 - beta_first) * scaled
    second_next = beta_second * second + (1.0 - beta_second) * scaled * scaled
    corrected = moment_next / (1.0 - beta_first**STEP)
    spread = jnp.sqrt(second_next / (1.0 - beta_second**STEP))
    update = corrected / (spread + epsilon)
    master_next = master - learn_rate * (update + decay * master)
    return (master_next, moment_next, second_next)


def squares_of(first, second):
    return jnp.sum(first * first) + jnp.sum(second * second)


def body(
    grads_matrix,
    grads_vector,
    master_matrix,
    master_vector,
    moment_matrix,
    moment_vector,
    second_matrix,
    second_vector,
):
    local_matrix = grads_matrix[0, 0].astype(jnp.float32)
    local_vector = grads_vector[0, 0].astype(jnp.float32)
    width = local_vector.shape[1]
    count = 3 * width * width + 5 * width
    part_matrix, part_vector = (
        lax.psum_scatter(
            local_matrix.astype(jnp.bfloat16), "shard", scatter_dimension=1, tiled=True
        ).astype(jnp.float32),
        lax.psum_scatter(
            local_vector.astype(jnp.bfloat16), "shard", scatter_dimension=1, tiled=True
        ).astype(jnp.float32),
    )
    mine_matrix, mine_vector = (
        lax.psum(part_matrix.astype(jnp.bfloat16), "rep").astype(jnp.float32),
        lax.psum(part_vector.astype(jnp.bfloat16), "rep").astype(jnp.float32),
    )
    squares = lax.psum(squares_of(mine_matrix, mine_vector), "shard")
    clip = jnp.minimum(1.0, 1.0 / jnp.sqrt(squares / count + 1e-06))
    master_mat, moment_mat, second_mat = adam_piece(
        mine_matrix, master_matrix, moment_matrix, second_matrix, clip, decay_rate
    )
    master_vec, moment_vec, second_vec = adam_piece(
        mine_vector, master_vector, moment_vector, second_vector, clip, 0.0
    )
    weights_mat, weights_vec = (
        lax.all_gather(master_mat.astype(jnp.bfloat16), "shard", axis=1, tiled=True),
        lax.all_gather(master_vec.astype(jnp.bfloat16), "shard", axis=1, tiled=True),
    )
    return (
        master_mat,
        master_vec,
        moment_mat,
        moment_vec,
        second_mat,
        second_vec,
        weights_mat,
        weights_vec,
    )


def solution(mesh):
    return jax.shard_map(
        body,
        mesh=mesh,
        in_specs=(
            P("rep", "shard", None, None, None),
            P("rep", "shard", None, None),
            P(None, "shard", None),
            P(None, "shard"),
            P(None, "shard", None),
            P(None, "shard"),
            P(None, "shard", None),
            P(None, "shard"),
        ),
        out_specs=(
            P(None, "shard", None),
            P(None, "shard"),
            P(None, "shard", None),
            P(None, "shard"),
            P(None, "shard", None),
            P(None, "shard"),
            P(),
            P(),
        ),
        check_vma=False,
    )
```

profile of v0, /device:TPU:1, one launch (start us, length us, event | category | flops | bytes accessed | tf_op | source)
XLA Modules:
  0.0 355.9 jit_solution(2101009983233991101)
XLA Ops:
  7.2 0.0 reduce-scatter.3.cloned.1.call-start
  7.2 0.7 reduce-scatter.3.cloned.1.call-update
  7.9 0.0 copy-start
  7.9 0.0 reduce-scatter.5.cloned.1.call-start
  8.0 0.7 reduce-scatter.5.cloned.1.call-update
  8.7 0.0 all-reduce.2.cloned.1.call-start
  8.7 114.5 %reduce-scatter.3.cloned.1.call-done = bf16[3,256,1024]{2,1,0:T(8,128)(2,1)} async-done(((bf16[3,1024,1024]{2,1,0:T(8,128)(2,1)}), bf16[3,256,1024]{2,1,0:T(8,128)(2,1)}) %reduce-scatter.3.cloned.1.call-update) | async-done | bytes 1572880 | tf_op jit(solution)/shard_map/reduce_scatter | solution.py:46
  123.2 0.0 all-reduce.2.cloned.1.call-update
  123.2 0.0 all-gather.2.cloned.1.call-start
  123.3 19.3 %reduce-scatter.5.cloned.1.call-done = bf16[5,256]{1,0:T(8,128)(2,1)} async-done(((bf16[5,1024]{1,0:T(8,128)(2,1)}), bf16[5,256]{1,0:T(8,128)(2,1)}) %reduce-scatter.5.cloned.1.call-update) | async-done | bytes 2576 | tf_op jit(solution)/shard_map/reduce_scatter | solution.py:49
  142.6 14.2 %psum.22 = bf16[5,256]{1,0:T(8,128)(2,1)S(1)} all-reduce(bf16[5,256]{1,0:T(8,128)(2,1)} %reduce-scatter.5.cloned.1.call-done), channel_id=1, replica_groups=mesh['rep'=8,'shard'=4] {'rep'}, use_global_device_ids=true, to_apply=%region_4.0 | all-reduce | flops 1280 | bytes 5120 | tf_op jit(solution)/shard_map/psum | solution.py:55
  156.8 0.6 fusion.6
  157.4 47.2 %all-reduce.2.cloned.1.call-done = bf16[3,256,1024]{2,1,0:T(8,128)(2,1)} async-done(((bf16[3,256,1024]{2,1,0:T(8,128)(2,1)}), bf16[3,256,1024]{2,1,0:T(8,128)(2,1)}) %all-reduce.2.cloned.1.call-update) | async-done | bytes 1572880 | tf_op jit(solution)/shard_map/psum | solution.py:54
  204.6 2.8 fusion.2
  208.7 10.2 %psum.23 = f32[]{:T(128)} all-reduce(f32[]{:T(128)S(6)} %add.46), channel_id=1, replica_groups=mesh['rep'=8,'shard'=4] {'shard'}, use_global_device_ids=true, to_apply=%region_6.0 | all-reduce | flops 1 | bytes 8 | tf_op jit(solution)/shard_map/psum | solution.py:57
  219.6 0.0 copy-done
  219.6 0.0 copy-start.1
  219.6 0.0 copy-start.2
  219.6 0.0 copy-start.3
  219.6 7.5 %fusion.11 = (bf16[3,256,1024]{2,1,0:T(8,128)(2,1)}, f32[3,256,1024]{2,1,0:T(8,128)}, f32[3,256,1024]{2,1,0:T(8,128)}, f32[3,256,1024]{2,1,0:T(8,128)}) fusion(f32[3,256,1024]{2,1,0:T(8,128)S(1)} %copy-done, f32[]{:T(128)S(6)} %min.3, bf16[3,256,1024]{2,1,0:T(8,128)(2,1)} %all-reduce.2.cloned.1.call-done, f32[3,256,1024]{2,1,0:T(8,128)} %param.14, ...), kind=kLoop, calls=%fused_computation.17 | loop fusion | flops 13369344 | bytes 22020100 | tf_op jit(solution)/shard_map/convert_element_type | solution.py:66
  227.1 0.0 all-gather.2.cloned.1.call-update
  227.2 0.0 copy-done.1
  227.2 0.0 copy-done.2
  227.2 0.0 copy-done.3
  227.2 0.6 fusion.8
  227.8 10.2 %all_gather.7 = bf16[5,1024]{1,0:T(8,128)(2,1)S(1)} all-gather(bf16[5,256]{1,0:T(8,128)(2,1)S(1)} %get-tuple-element.8), channel_id=1, replica_groups=mesh['rep'=8,'shard'=4] {'shard'}, dimensions={1}, use_global_device_ids=true | all-gather | bytes 12800 | tf_op jit(solution)/shard_map/all_gather | solution.py:67
  238.0 104.5 %all-gather.2.cloned.1.call-done = bf16[3,1024,1024]{2,1,0:T(8,128)(2,1)} async-done(((bf16[3,256,1024]{2,1,0:T(8,128)(2,1)}), bf16[3,1024,1024]{2,1,0:T(8,128)(2,1)}) %all-gather.2.cloned.1.call-update) | async-done | bytes 6291472 | tf_op jit(solution)/shard_map/all_gather | solution.py:66
  342.5 6.2 %copy.19 = bf16[3,1024,1024]{2,1,0:T(8,128)(2,1)} copy(bf16[3,1024,1024]{2,1,0:T(8,128)(2,1)} %all-gather.2.cloned.1.call-done) | data formatting | bytes 12582912
  348.7 0.6 copy.20
Async XLA Ops:
  7.2 116.0 %reduce-scatter.3.cloned.1.call-start = ((), (), s32[]{:S(2)}) async-start(), calls=%async_computation.2 | async-start | bytes 7864320 | tf_op jit(solution)/shard_map/reduce_scatter | solution.py:46
  7.9 211.7 %copy-start = (f32[3,256,1024]{2,1,0:T(8,128)S(1)}, f32[3,256,1024]{2,1,0:T(8,128)}, u32[]{:S(2)}) copy-start(f32[3,256,1024]{2,1,0:T(8,128)} %param.10) | copy-start | bytes 9437188
  7.9 134.7 %reduce-scatter.5.cloned.1.call-start = ((), (), s32[]{:S(2)}) async-start(), calls=%async_computation.4 | async-start | bytes 20480 | tf_op jit(solution)/shard_map/reduce_scatter | solution.py:49
  8.7 195.9 %all-reduce.2.cloned.1.call-start = ((), (), s32[]{:S(2)}) async-start(), calls=%async_computation.3 | async-start | bytes 3145728 | tf_op jit(solution)/shard_map/psum | solution.py:54
  123.2 219.3 %all-gather.2.cloned.1.call-start = ((), (), s32[]{:S(2)}) async-start(), calls=%async_computation.5 | async-start | bytes 7864320 | tf_op jit(solution)/shard_map/all_gather | solution.py:66
  219.6 7.6 %copy-start.1 = (f32[5,256]{1,0:T(8,128)S(1)}, f32[5,256]{1,0:T(8,128)}, u32[]{:S(2)}) copy-start(f32[5,256]{1,0:T(8,128)} %param.11) | copy-start | bytes 15364
  219.6 7.6 %copy-start.2 = (f32[5,256]{1,0:T(8,128)S(1)}, f32[5,256]{1,0:T(8,128)}, u32[]{:S(2)}) copy-start(f32[5,256]{1,0:T(8,128)} %param.15) | copy-start | bytes 15364
  219.6 7.6 %copy-start.3 = (f32[5,256]{1,0:T(8,128)S(1)}, f32[5,256]{1,0:T(8,128)}, u32[]{:S(2)}) copy-start(f32[5,256]{1,0:T(8,128)} %param.13) | copy-start | bytes 15364
Sparse Core Ops, SparseCore 0:
  10.3 112.8 reduce-scatter.2
  125.4 17.1 reduce-scatter.4
  146.2 58.3 all-reduce.1
  227.3 115.1 all-gather.1
where the time goes:
time: 357 us; the launch traced here: 356 us
  waiting for transfers between devices  287 us (80%)
  blocking collectives  34.6 us (10%)
  between operations  15.8 us (4%)
  other arithmetic  11.6 us (3%)
  local copies, waits for them, and re-layouts  6.82 us (2%)
    reduce_scatter x1, waiting for transfers between devices, body(): lax.psum_scatter(local_matrix.astype(jnp.bfloat16), 'shard', scatter_dime...  114 us
    all_gather x1, waiting for transfers between devices, body(): lax.all_gather(master_mat.astype(jnp.bfloat16), 'shard', axis=1, tiled=True)  104 us
    psum x1, waiting for transfers between devices, body(): lax.psum(part_matrix.astype(jnp.bfloat16), 'rep').astype(jnp.float32)  47.2 us
    reduce_scatter x1, waiting for transfers between devices, body(): lax.psum_scatter(local_vector.astype(jnp.bfloat16), 'shard', scatter_dime...  19.3 us
    psum x1, blocking collectives, body(): lax.psum(part_vector.astype(jnp.bfloat16), 'rep').astype(jnp.float32)  14.2 us
    all_gather x1, blocking collectives, body(): lax.all_gather(master_vec.astype(jnp.bfloat16), 'shard', axis=1, tiled=True)  10.2 us
    psum x1, blocking collectives, body(): squares = lax.psum(squares_of(mine_matrix, mine_vector), 'shard')  10.2 us
    convert_element_type x1, other arithmetic, body(): master_mat.astype(jnp.bfloat16)  7.51 us
  transfers between devices with their start and end apart: 4, of which 4 were waited for; matrix products, arithmetic and copies ran while one was open for 0% of the time, Pallas kernels for 0%

commit v1 on v0

v1 whole, which is shorter than its diff:
```python
import functools
import math

import jax
import jax.numpy as jnp
from jax import lax
from jax.experimental import pallas as pl
from jax.experimental.pallas import tpu as pltpu
from jax.sharding import PartitionSpec as P

STEP = 1000


beta_first = 0.9
beta_second = 0.999
learn_rate = 0.01
decay_rate = 0.1
epsilon = 1e-08

SPLIT = 1


def adam_piece(total, master, moment, second, clip, decay):
    scaled = total * clip
    moment_next = beta_first * moment + (1.0 - beta_first) * scaled
    second_next = beta_second * second + (1.0 - beta_second) * scaled * scaled
    corrected = moment_next / (1.0 - beta_first**STEP)
    spread = jnp.sqrt(second_next / (1.0 - beta_second**STEP))
    update = corrected / (spread + epsilon)
    master_next = master - learn_rate * (update + decay * master)
    return (master_next, moment_next, second_next)


def kernel(
    R, S, count,
    gm, gv, mm, mv, om, ov, sm, sv,
    wout, tot, clip_out, vtot, vecw,
    acc, rC, rX, rZ, wp, wq, vbuf, rV, sq, sqs, rS, vmine,
    bm, bo, bs,
    lsem, csem, xsem, zsem, gsem, vsem, ssem, wzsem, wgsem, wvsem, psem, osem,
):
    f32, bf16 = jnp.float32, jnp.bfloat16
    n = int(math.log2(R))
    M, _, Q, W = gm.shape
    half = W // 2
    cw = half // SPLIT
    K = M * SPLIT
    r = lax.axis_index("rep")
    z = lax.axis_index("shard")
    core = r % 2
    bits, partners = [], []
    for i in range(n - 1):
        lo, hi = 2 << i, 1 << (n - 1 - i)
        mask = lo + core * (hi - lo)
        bit = (1 - core) * ((r // lo) % 2) + core * ((r // hi) % 2)
        bits.append(bit)
        partners.append(r + (1 - 2 * bit) * mask)
    twin = r + 1 - 2 * core
    sizes = [Q >> i for i in range(n)]
    offs = [0]
    for i in range(n - 1):
        offs.append(offs[-1] + bits[i] * sizes[i + 1])
    al = sizes[n - 1]
    pr = sizes[n - 1]

    def mul(x, m):
        return x if isinstance(x, int) else pl.multiple_of(x, m)

    off = [mul(o, al) for o in offs]
    mycol = lambda j: pl.ds(pl.multiple_of(core * half + j * cw, cw), cw)
    otcol = lambda j: pl.ds(pl.multiple_of((1 - core) * half + j * cw, cw), cw)
    myhalf = pl.ds(pl.multiple_of(core * half, half), half)
    zpeer = [lax.rem(z + d, S) for d in range(S)]
    zfrom = [lax.rem(z + S - d, S) for d in range(S)]

    sends = []

    def remote(src, dst, ss, rs, rep=None, shard=None):
        where = {"rep": rep} if shard is None else {"shard": shard}
        cp = pltpu.make_async_remote_copy(
            src_ref=src, dst_ref=dst, send_sem=ss, recv_sem=rs,
            device_id=where, device_id_type=pl.DeviceIdType.MESH,
        )
        cp.start()
        sends.append(cp)
        return cp

    barrier = pltpu.get_barrier_semaphore()
    for p in [twin] + partners:
        pl.semaphore_signal(barrier, inc=1, device_id={"rep": p}, device_id_type=pl.DeviceIdType.MESH)
    for d in range(1, S):
        pl.semaphore_signal(barrier, inc=1, device_id={"shard": zpeer[d]}, device_id_type=pl.DeviceIdType.MESH)

    locs = []
    for k in range(K):
        m, j = k // SPLIT, k % SPLIT
        cp = pltpu.make_async_copy(gm.at[m, :, :, mycol(j)], acc.at[k], lsem.at[k])
        cp.start()
        locs.append(cp)
    vbuf[...] = jnp.zeros_like(vbuf)
    vbuf[0, 0:5, :] = gv[...].astype(f32)
    pl.semaphore_wait(barrier, n + S - 1)

    cC = []
    for k in range(K):
        m, j = k // SPLIT, k % SPLIT
        cC.append(remote(gm.at[m, :, :, otcol(j)], rC.at[k], csem.at[0, k], csem.at[1, k], rep=twin))
    cV = {0: [remote(vbuf.at[0], rV.at[0], vsem.at[0, 0], vsem.at[1, 0], rep=twin)]}
    ins = []
    for i, (a, b) in enumerate(((mm, bm), (om, bo), (sm, bs))):
        cp = pltpu.make_async_copy(a, b, psem.at[i])
        cp.start()
        ins.append(cp)

    def add_rows(k, recv, start, size, base):
        step = min(size, 64)

        @pl.loop(0, S)
        def _(s):
            for b in range(size // step):
                rows = pl.ds(mul(start + b * step, 16), step)
                theirs = pl.ds(mul(start - base + b * step, 16), step)
                acc[k, s, rows, :] = (acc[k, s, rows, :].astype(f32) + recv[s, theirs, :].astype(f32)).astype(bf16)

    cX, cZ, cG = {}, {}, {}
    other = [mul(offs[i] + (1 - bits[i]) * sizes[i + 1], al) for i in range(n - 1)]

    def stage(k, st):
        m, j = k // SPLIT, k % SPLIT
        if st < n:
            if st == 0:
                locs[k].wait()
                cC[k].wait_recv()
                recv, base = rC.at[k], 0
            else:
                cX[k, st - 1].wait_recv()
                recv, base = rX[st - 1].at[k], offs[st]
            if st < n - 1:
                add_rows(k, recv, other[st], sizes[st + 1], base)
                cX[k, st] = remote(
                    acc.at[k, :, pl.ds(other[st], sizes[st + 1]), :], rX[st].at[k],
                    xsem.at[0, k, st], xsem.at[1, k, st], rep=partners[st])
                add_rows(k, recv, off[st + 1], sizes[st + 1], base)
            else:
                add_rows(k, recv, off[st], sizes[st], base)
                for d in range(1, S):
                    cZ[k, d] = remote(
                        acc.at[k, zpeer[d], pl.ds(off[st], pr), :], rZ.at[k, d - 1],
                        zsem.at[0, k, d - 1], zsem.at[1, k, d - 1], shard=zpeer[d])
        elif st == n:
            own = acc[k, z, pl.ds(off[n - 1], pr), :].astype(f32)
            for d in range(1, S):
                cZ[k, d].wait_recv()
                own = own + rZ[k, d - 1].astype(f32)
            tot[m, pl.ds(off[n - 1], pr), mycol(j)] = own.astype(bf16)
            send_total(k, n - 1)
        elif st < 2 * n:
            i = 2 * n - 1 - st
            cG[k, i + 1].wait_recv()
            send_total(k, i)
        else:
            cG[k, 0].wait_recv()
            for c in range(2):
                @pl.loop(0, Q // 32)
                def _(b):
                    x = tot[m, pl.ds(pl.multiple_of(b * 32, 32), 32), c * half + j * cw : c * half + (j + 1) * cw].astype(f32)
                    x = x * x
                    t = x[0:8] + x[8:16] + x[16:24] + x[24:32]
                    for q in range(cw // 128):
                        sq[:, q * 128 : (q + 1) * 128] += t[:, q * 128 : (q + 1) * 128]

    def send_total(k, i):
        m, j = k // SPLIT, k % SPLIT
        part = tot.at[m, pl.ds(off[i], sizes[i]), mycol(j)]
        to = partners[i - 1] if i else twin
        cG[k, i] = remote(part, part, gsem.at[0, k, i], gsem.at[1, k, i], rep=to)

    def vec_stage(t):
        if t < n:
            cV[t][0].wait_recv()
            vbuf[t + 1] = vbuf[t] + rV[t]
            if t < n - 1:
                cV[t + 1] = [remote(vbuf.at[t + 1], rV.at[t + 1], vsem.at[0, t + 1], vsem.at[1, t + 1], rep=partners[t])]
            else:
                cV[n] = [remote(vbuf.at[n], rV.at[n + d - 1], vsem.at[0, n + d - 1], vsem.at[1, n + d - 1], shard=zpeer[d]) for d in range(1, S)]
        elif t == n:
            total = vbuf[n]
            for d in range(1, S):
                cV[n][d - 1].wait_recv()
                total = total + rV[n + d - 1]
            vbuf[n + 1] = total

    sq[...] = jnp.zeros_like(sq)
    last = 2 * n
    for t in range(K + last):
        for st in range(last, -1, -1):
            k = t - st
            if 0 <= k < K:
                stage(k, st)
        vec_stage(t)

    sums = sq[:, 0:128]
    for q in range(1, cw // 128):
        sums = sums + sq[:, q * 128 : (q + 1) * 128]
    sqs[...] = sums
    cS = [remote(sqs, rS.at[d - 1], ssem.at[0, d - 1], ssem.at[1, d - 1], shard=zpeer[d]) for d in range(1, S)]
    for cp in ins:
        cp.wait()
    vt = vbuf[n + 1]
    vsq = jnp.sum(vt * vt, keepdims=True)
    for d in range(1, S):
        cS[d - 1].wait_recv()
        sums = sums + rS[d - 1]
    squares = jnp.sum(sums, keepdims=True) + vsq
    clip = jnp.minimum(1.0, 1.0 / jnp.sqrt(squares / count + 1e-06))
    clip_out[...] = jnp.broadcast_to(clip, clip_out.shape)

    def weights(m, rows, cols):
        return adam_piece(tot[m, rows, cols].astype(f32), bm[m, rows, cols], bo[m, rows, cols], bs[m, rows, cols], clip, decay_rate)[0].astype(bf16)

    wZ, wG = {}, {}
    for m in range(M):
        @pl.loop(0, pr // 16)
        def _(b):
            b16 = pl.multiple_of(b * 16, 16)
            wp[m, pl.ds(b16, 16), :] = weights(m, pl.ds(mul(off[n - 1] + b16, 16), 16), myhalf)

        for d in range(1, S):
            wZ[m, d] = remote(
                wp.at[m], wout.at[m, z, pl.ds(off[n - 1], pr), myhalf],
                wzsem.at[0, m, d - 1], wzsem.at[1, m, d - 1], shard=zpeer[d])
    mycols = pl.ds(pl.multiple_of(z * vmine.shape[1], 128), vmine.shape[1])
    vown = vbuf[n + 1, :, mycols]
    vtot[...] = vown
    vmine[...] = jnp.zeros_like(vmine)
    vmine[0:5, :] = adam_piece(vown[0:5], mv[...], ov[...], sv[...], clip, 0.0)[0]
    wV = [remote(vmine, vecw.at[:, mycols], wvsem.at[0, d - 1], wvsem.at[1, d - 1], shard=zpeer[d]) for d in range(1, S)]
    vecw[:, mycols] = vmine[...]

    outs = []
    for m in range(M):
        @pl.loop(0, Q // 16)
        def _(b):
            rows = pl.ds(pl.multiple_of(b * 16, 16), 16)
            wq[m, rows, :] = weights(m, rows, slice(None))
        cp = pltpu.make_async_copy(wq.at[m], wout.at[m, z], osem.at[m])
        cp.start()
        outs.append(cp)

    units = [(m, d) for m in range(M) for d in range(1, S)]

    def spread(u, st):
        m, d = units[u]
        if st == 0:
            wZ[m, d].wait_recv()
        else:
            wG[u, n - st].wait_recv()
        if st < n:
            i = n - 1 - st
            part = wout.at[m, zfrom[d], pl.ds(off[i], sizes[i]), myhalf]
            wG[u, i] = remote(part, part, wgsem.at[0, u, i], wgsem.at[1, u, i], rep=partners[i - 1] if i else twin)

    for t in range(len(units) + n):
        for st in range(n, -1, -1):
            u = t - st
            if 0 <= u < len(units):
                spread(u, st)
    for cp in wV:
        cp.wait_recv()
    for cp in outs:
        cp.wait()
    for cp in sends:
        cp.wait_send()


def body(
    R, S,
    grads_matrix,
    grads_vector,
    master_matrix,
    master_vector,
    moment_matrix,
    moment_vector,
    second_matrix,
    second_vector,
):
    f32, bf16 = jnp.float32, jnp.bfloat16
    M, D, W = grads_matrix.shape[2:]
    V = grads_vector.shape[2]
    Q = D // S
    n = int(math.log2(R))
    count = M * D * W + V * W
    half = W // 2
    cw = half // SPLIT
    K = M * SPLIT
    pr = Q >> (n - 1)
    U = M * (S - 1)
    dma = pltpu.SemaphoreType.DMA
    anyspec = pl.BlockSpec(memory_space=pl.ANY)
    vspec = pl.BlockSpec(memory_space=pltpu.VMEM)
    wout, tot, clip, vtot, vecw = pl.pallas_call(
        functools.partial(kernel, R, S, count),
        out_shape=(
            jax.ShapeDtypeStruct((M, S, Q, W), bf16),
            jax.ShapeDtypeStruct((M, Q, W), bf16),
            jax.ShapeDtypeStruct((8, 128), f32),
            jax.ShapeDtypeStruct((8, W // S), f32),
            jax.ShapeDtypeStruct((8, W), f32),
        ),
        in_specs=[anyspec, vspec, anyspec, vspec, anyspec, vspec, anyspec, vspec],
        out_specs=(anyspec, vspec, vspec, vspec, vspec),
        scratch_shapes=[
            pltpu.VMEM((K, S, Q, cw), bf16),
            pltpu.VMEM((K, S, Q, cw), bf16),
            [pltpu.VMEM((K, S, Q >> (i + 1), cw), bf16) for i in range(n - 1)],
            pltpu.VMEM((K, S - 1, pr, cw), bf16),
            pltpu.VMEM((M, pr, half), bf16),
            pltpu.VMEM((M, Q, W), bf16),
            pltpu.VMEM((n + 2, 8, W), f32),
            pltpu.VMEM((n + S - 1, 8, W), f32),
            pltpu.VMEM((8, cw), f32),
            pltpu.VMEM((8, 128), f32),
            pltpu.VMEM((S - 1, 8, 128), f32),
            pltpu.VMEM((8, W // S), f32),
            pltpu.VMEM((M, Q, W), f32),
            pltpu.VMEM((M, Q, W), f32),
            pltpu.VMEM((M, Q, W), f32),
            dma((K,)),
            dma((2, K)),
            dma((2, K, n - 1)),
            dma((2, K, S - 1)),
            dma((2, K, n)),
            dma((2, n + S - 1)),
            dma((2, S - 1)),
            dma((2, M, S - 1)),
            dma((2, U, n)),
            dma((2, S - 1)),
            dma((3,)),
            dma((M,)),
        ],
        compiler_params=pltpu.CompilerParams(
            collective_id=0, has_side_effects=True, vmem_limit_bytes=56 * 1024 * 1024
        ),
    )(
        grads_matrix.reshape(M, S, Q, W),
        grads_vector.reshape(V, W),
        master_matrix, master_vector, moment_matrix, moment_vector, second_matrix, second_vector,
    )
    factor = clip[0, 0]
    master_mat, moment_mat, second_mat = adam_piece(
        tot.astype(f32), master_matrix, moment_matrix, second_matrix, factor, decay_rate
    )
    master_vec, moment_vec, second_vec = adam_piece(
        vtot[:V], master_vector, moment_vector, second_vector, factor, 0.0
    )
    return (
        master_mat,
        master_vec,
        moment_mat,
        moment_vec,
        second_mat,
        second_vec,
        wout.reshape(M, D, W),
        vecw[:V].astype(bf16),
    )


def solution(mesh):
    R, S = mesh.shape["rep"], mesh.shape["shard"]
    return jax.shard_map(
        functools.partial(body, R, S),
        mesh=mesh,
        in_specs=(
            P("rep", "shard", None, None, None),
            P("rep", "shard", None, None),
            P(None, "shard", None),
            P(None, "shard"),
            P(None, "shard", None),
            P(None, "shard"),
            P(None, "shard", None),
            P(None, "shard"),
        ),
        out_specs=(
            P(None, "shard", None),
            P(None, "shard"),
            P(None, "shard", None),
            P(None, "shard"),
            P(None, "shard", None),
            P(None, "shard"),
            P(),
            P(),
        ),
        check_vma=False,
    )
```

time: 357 us -> 131 us (0.37)
  waiting for transfers between devices: 287 us -> 0 us
  Pallas kernels: 0 us -> 115 us
  blocking collectives: 34.6 us -> 0 us
  between operations: 15.8 us -> 0.71 us
    reduce_scatter x2 -> x0, waiting for transfers between devices: 134 us -> none  [the longest x1 114 us: body(): lax.psum_scatter(local_matrix.astype(jnp.bfloat16), 'shard', scatter_dime...]
    pallas_call x0 -> x1, Pallas kernels: none -> 115 us  [body(): pl.pallas_call(functools.partial(kernel, R, S, count), out_shape=(jax.Sha...]
    all_gather x1 -> x0, waiting for transfers between devices: 104 us -> none  [body(): lax.all_gather(master_mat.astype(jnp.bfloat16), 'shard', axis=1, tiled=True)]
    psum x1 -> x0, waiting for transfers between devices: 47.2 us -> none  [body(): lax.psum(part_matrix.astype(jnp.bfloat16), 'rep').astype(jnp.float32)]
    psum x2 -> x0, blocking collectives: 24.4 us -> none  [the longest x1 14.2 us: body(): lax.psum(part_vector.astype(jnp.bfloat16), 'rep').astype(jnp.float32)]
    all_gather x1 -> x0, blocking collectives: 10.2 us -> none  [body(): lax.all_gather(master_vec.astype(jnp.bfloat16), 'shard', axis=1, tiled=True)]
    sub x0 -> x2, other arithmetic: none -> 9.74 us  [adam_piece(): master_next = master - learn_rate * (update + decay * master)]
    convert_element_type x2 -> x0, other arithmetic: 8.14 us -> none  [the longest x1 7.51 us: body(): master_mat.astype(jnp.bfloat16)]
  transfers between devices with their start and end apart: 4 -> 0, of which waited for: 4 -> 0; matrix products, arithmetic and copies ran while one was open for 0% -> 0% of each run, Pallas kernels for 0% -> 0%
where the time goes in v1:
time: 131 us
  Pallas kernels  115 us (88%)
  other arithmetic  9.74 us (7%)
  local copies, waits for them, and re-layouts  5.29 us (4%)
    pallas_call x1, Pallas kernels, body(): pl.pallas_call(functools.partial(kernel, R, S, count), out_shape=(jax.Sha...  115 us
    sub x2, other arithmetic, adam_piece(): master_next = master - learn_rate * (update + decay * master)  9.74 us
    unnamed x15, local copies, waits for them, and re-layouts  2.74 us

profile of v1, /device:TPU:1, one launch (start us, length us, event | category | flops | bytes accessed | tf_op | source)
XLA Modules:
  0.0 130.7 jit_solution(14347112069179871968)
XLA Ops:
  0.6 0.0 copy-start.2
  0.6 0.0 copy-start.3
  0.7 0.0 copy-start.4
  0.7 0.0 copy-start
  0.7 0.0 copy-start.1
  0.7 115.0 %shard_map.143 = (bf16[3,4,256,1024]{3,2,1,0:T(8,128)(2,1)}, bf16[3,256,1024]{2,1,0:T(8,128)(2,1)}, f32[8,128]{1,0:T(8,128)}, f32[8,256]{1,0:T(8,128)}, f32[8,1024]{1,0:T(8,128)}) custom-call(bf16[3,4,256,1024]{3,2,1,0:T(8,128)(2,1)} %bitcast.4, bf16[5,1024]{1,0:T(8,128)(2,1)} %bitcast.8, f32[3,256,1024]{2,1,0:T(8,128)} %mm.1, f32[5,256]{1,0:T(8,128)} %mv.1, ...), custom_call_target="tpu_custom_call" | custom-call | tf_op jit(solution)/shard_map/pallas_call | solution.py:301
  115.7 1.2 slice.10
  116.9 1.4 %slice.20 = bf16[5,1024]{1,0:T(8,128)(2,1)} slice(f32[8,1024]{1,0:T(8,128)} %get-tuple-element.17), slice={[0:5], [0:1024]} | slice | bytes 20480 | tf_op jit(solution)/shard_map/slice | solution.py:364
  118.2 0.0 copy-done.2
  118.2 0.0 copy-done.3
  118.2 0.0 copy-done.4
  118.2 2.0 %multiply_subtract_fusion.1 = (f32[5,256]{1,0:T(8,128)}, f32[5,256]{1,0:T(8,128)}, f32[5,256]{1,0:T(8,128)}) fusion(f32[5,256]{1,0:T(8,128)S(1)} %copy-done.2, f32[]{:T(128)} %bitcast.2, f32[8,256]{1,0:T(8,128)} %get-tuple-element.15, f32[5,256]{1,0:T(8,128)S(1)} %copy-done.4, f32[5,256]{1,0:T(8,128)S(1)} %copy-done.3), kind=kLoop, calls=%fused_computation.8 | loop fusion | flops 19200 | bytes 35844 | tf_op jit(solution)/shard_map/sub | solution.py:30
  120.2 0.0 slice-start
  120.2 0.0 copy-done
  120.2 0.0 copy-done.1
  120.2 0.0 slice-start.1
  120.2 7.8 %multiply_subtract_fusion = (f32[3,256,1024]{2,1,0:T(8,128)}, f32[3,256,1024]{2,1,0:T(8,128)}, f32[3,256,1024]{2,1,0:T(8,128)}) fusion(f32[3,256,1024]{2,1,0:T(8,128)S(1)} %copy-done, f32[]{:T(128)} %bitcast.2, bf16[3,256,1024]{2,1,0:T(8,128)(2,1)} %get-tuple-element.13, f32[3,256,1024]{2,1,0:T(8,128)} %sm.1, f32[3,256,1024]{2,1,0:T(8,128)S(1)} %copy-done.1), kind=kLoop, calls=%fused_computation.2 | loop fusion | flops 12582912 | bytes 20447236 | tf_op jit(solution)/shard_map/sub | solution.py:30
  128.0 0.0 slice-done
  128.0 0.0 slice-done.1
  128.0 2.7 %copy.17 = bf16[3,1024,1024]{2,1,0:T(8,128)(2,1)} copy(bf16[3,1024,1024]{2,1,0:T(8,128)(2,1)S(1)} %bitcast.7) | data formatting | bytes 12582912
  (1 shorter events, 0.0 us)
Async XLA Ops:
  0.6 117.6 %copy-start.2 = (f32[5,256]{1,0:T(8,128)S(1)}, f32[5,256]{1,0:T(8,128)}, u32[]{:S(2)}) copy-start(f32[5,256]{1,0:T(8,128)} %mv.1) | copy-start | bytes 15364
  0.6 117.6 %copy-start.3 = (f32[5,256]{1,0:T(8,128)S(1)}, f32[5,256]{1,0:T(8,128)}, u32[]{:S(2)}) copy-start(f32[5,256]{1,0:T(8,128)} %ov.1) | copy-start | bytes 15364
  0.7 117.6 %copy-start.4 = (f32[5,256]{1,0:T(8,128)S(1)}, f32[5,256]{1,0:T(8,128)}, u32[]{:S(2)}) copy-start(f32[5,256]{1,0:T(8,128)} %sv.1) | copy-start | bytes 15364
  0.7 119.5 %copy-start = (f32[3,256,1024]{2,1,0:T(8,128)S(1)}, f32[3,256,1024]{2,1,0:T(8,128)}, u32[]{:S(2)}) copy-start(f32[3,256,1024]{2,1,0:T(8,128)} %mm.1) | copy-start | bytes 9437188
  0.7 119.5 %copy-start.1 = (f32[3,256,1024]{2,1,0:T(8,128)S(1)}, f32[3,256,1024]{2,1,0:T(8,128)}, u32[]{:S(2)}) copy-start(f32[3,256,1024]{2,1,0:T(8,128)} %om.1) | copy-start | bytes 9437188
  120.2 7.8 %slice-start = ((s8[6291456]{0:T(1024)(128)(4,1)}), s8[4194304]{0:T(1024)(128)(4,1)S(1)}, s32[]{:S(2)}) async-start(s8[6291456]{0:T(1024)(128)(4,1)} %bitcast.5), calls=%async_computation | async-start | bytes 8388608
  120.2 7.8 %slice-start.1 = ((s8[6291456]{0:T(1024)(128)(4,1)}), s8[2097152]{0:T(1024)(128)(4,1)S(1)}, s32[]{:S(2)}) async-start(s8[6291456]{0:T(1024)(128)(4,1)} %bitcast.5), calls=%async_computation.1 | async-start | bytes 4194304

commit v2 on v1

--- a/solution.py
+++ b/solution.py
@@ -34,10 +34,9 @@
 def kernel(
     R, S, count,
     gm, gv, mm, mv, om, ov, sm, sv,
-    wout, tot, clip_out, vtot, vecw,
-    acc, rC, rX, rZ, wp, wq, vbuf, rV, sq, sqs, rS, vmine,
-    bm, bo, bs,
-    lsem, csem, xsem, zsem, gsem, vsem, ssem, wzsem, wgsem, wvsem, psem, osem,
+    bm, bv, bo, bov, bs, bsv, wout, vout,
+    tot, vecw, acc, rC, rX, rZ, wp, vbuf, rV, sq, sqs, rS, vmine,
+    lsem, csem, xsem, zsem, gsem, vsem, ssem, wzsem, wgsem, wvsem, psem,
 ):
     f32, bf16 = jnp.float32, jnp.bfloat16
     n = int(math.log2(R))
@@ -191,13 +190,17 @@
             vbuf[n + 1] = total
 
     sq[...] = jnp.zeros_like(sq)
-    last = 2 * n
-    for t in range(K + last):
-        for st in range(last, -1, -1):
-            k = t - st
-            if 0 <= k < K:
-                stage(k, st)
-        vec_stage(t)
+    order = []
+    for k in range(K):
+        first = 8 * (k + 1)
+        for st in range(2 * n + 1):
+            order.append((0 if st == 0 else first + 5 * (st - 1), k, st))
+    order += [(12 * t, K, t) for t in range(n + 1)]
+    for _, k, st in sorted(order):
+        if k < K:
+            stage(k, st)
+        else:
+            vec_stage(st)
 
     sums = sq[:, 0:128]
     for q in range(1, cw // 128):
@@ -213,7 +216,6 @@
         sums = sums + rS[d - 1]
     squares = jnp.sum(sums, keepdims=True) + vsq
     clip = jnp.minimum(1.0, 1.0 / jnp.sqrt(squares / count + 1e-06))
-    clip_out[...] = jnp.broadcast_to(clip, clip_out.shape)
 
     def weights(m, rows, cols):
         return adam_piece(tot[m, rows, cols].astype(f32), bm[m, rows, cols], bo[m, rows, cols], bs[m, rows, cols], clip, decay_rate)[0].astype(bf16)
@@ -231,21 +233,20 @@
                 wzsem.at[0, m, d - 1], wzsem.at[1, m, d - 1], shard=zpeer[d])
     mycols = pl.ds(pl.multiple_of(z * vmine.shape[1], 128), vmine.shape[1])
     vown = vbuf[n + 1, :, mycols]
-    vtot[...] = vown
     vmine[...] = jnp.zeros_like(vmine)
-    vmine[0:5, :] = adam_piece(vown[0:5], mv[...], ov[...], sv[...], clip, 0.0)[0]
+    bv[...], bov[...], bsv[...] = adam_piece(vown[0:5], mv[...], ov[...], sv[...], clip, 0.0)
+    vmine[0:5, :] = bv[...]
     wV = [remote(vmine, vecw.at[:, mycols], wvsem.at[0, d - 1], wvsem.at[1, d - 1], shard=zpeer[d]) for d in range(1, S)]
     vecw[:, mycols] = vmine[...]
 
-    outs = []
-    for m in range(M):
+    def update(m):
         @pl.loop(0, Q // 16)
         def _(b):
             rows = pl.ds(pl.multiple_of(b * 16, 16), 16)
-            wq[m, rows, :] = weights(m, rows, slice(None))
-        cp = pltpu.make_async_copy(wq.at[m], wout.at[m, z], osem.at[m])
-        cp.start()
-        outs.append(cp)
+            one, two, three = adam_piece(
+                tot[m, rows, :].astype(f32), bm[m, rows, :], bo[m, rows, :], bs[m, rows, :], clip, decay_rate)
+            bm[m, rows, :], bo[m, rows, :], bs[m, rows, :] = one, two, three
+            wout[m, z, rows, :] = one.astype(bf16)
 
     units = [(m, d) for m in range(M) for d in range(1, S)]
 
@@ -260,15 +261,17 @@
             part = wout.at[m, zfrom[d], pl.ds(off[i], sizes[i]), myhalf]
             wG[u, i] = remote(part, part, wgsem.at[0, u, i], wgsem.at[1, u, i], rep=partners[i - 1] if i else twin)
 
-    for t in range(len(units) + n):
-        for st in range(n, -1, -1):
-            u = t - st
-            if 0 <= u < len(units):
-                spread(u, st)
+    lag = [0, 2, 4, 5] if n == 3 else [2 * i for i in range(n + 1)]
+    order = [(u + lag[st], -st, u) for u in range(len(units)) for st in range(n + 1)]
+    order += [(2 * m + 1, -n - 1, m) for m in range(M)]
+    for _, st, u in sorted(order):
+        if st == -n - 1:
+            update(u)
+        else:
+            spread(u, -st)
     for cp in wV:
         cp.wait_recv()
-    for cp in outs:
-        cp.wait()
+    vout[...] = vecw[0:5, :].astype(bf16)
     for cp in sends:
         cp.wait_send()
 
@@ -296,35 +299,33 @@
     pr = Q >> (n - 1)
     U = M * (S - 1)
     dma = pltpu.SemaphoreType.DMA
-    anyspec = pl.BlockSpec(memory_space=pl.ANY)
     vspec = pl.BlockSpec(memory_space=pltpu.VMEM)
-    wout, tot, clip, vtot, vecw = pl.pallas_call(
+    hbm = pl.BlockSpec(memory_space=pltpu.HBM)
+    mat = jax.ShapeDtypeStruct((M, Q, W), f32)
+    vec = jax.ShapeDtypeStruct((V, W // S), f32)
+    master_mat, master_vec, moment_mat, moment_vec, second_mat, second_vec, wout, vout = pl.pallas_call(
         functools.partial(kernel, R, S, count),
         out_shape=(
+            mat, vec, mat, vec, mat, vec,
             jax.ShapeDtypeStruct((M, S, Q, W), bf16),
-            jax.ShapeDtypeStruct((M, Q, W), bf16),
-            jax.ShapeDtypeStruct((8, 128), f32),
-            jax.ShapeDtypeStruct((8, W // S), f32),
-            jax.ShapeDtypeStruct((8, W), f32),
+            jax.ShapeDtypeStruct((V, W), bf16),
         ),
-        in_specs=[anyspec, vspec, anyspec, vspec, anyspec, vspec, anyspec, vspec],
-        out_specs=(anyspec, vspec, vspec, vspec, vspec),
+        in_specs=[hbm, vspec, hbm, vspec, hbm, vspec, hbm, vspec],
+        out_specs=(vspec,) * 8,
         scratch_shapes=[
+            pltpu.VMEM((M, Q, W), bf16),
+            pltpu.VMEM((8, W), f32),
             pltpu.VMEM((K, S, Q, cw), bf16),
             pltpu.VMEM((K, S, Q, cw), bf16),
             [pltpu.VMEM((K, S, Q >> (i + 1), cw), bf16) for i in range(n - 1)],
             pltpu.VMEM((K, S - 1, pr, cw), bf16),
             pltpu.VMEM((M, pr, half), bf16),
-            pltpu.VMEM((M, Q, W), bf16),
             pltpu.VMEM((n + 2, 8, W), f32),
             pltpu.VMEM((n + S - 1, 8, W), f32),
             pltpu.VMEM((8, cw), f32),
             pltpu.VMEM((8, 128), f32),
             pltpu.VMEM((S - 1, 8, 128), f32),
             pltpu.VMEM((8, W // S), f32),
-            pltpu.VMEM((M, Q, W), f32),
-            pltpu.VMEM((M, Q, W), f32),
-            pltpu.VMEM((M, Q, W), f32),
             dma((K,)),
             dma((2, K)),
             dma((2, K, n - 1)),
@@ -336,22 +337,14 @@
             dma((2, U, n)),
             dma((2, S - 1)),
             dma((3,)),
-            dma((M,)),
         ],
         compiler_params=pltpu.CompilerParams(
-            collective_id=0, has_side_effects=True, vmem_limit_bytes=56 * 1024 * 1024
+            collective_id=0, has_side_effects=True, vmem_limit_bytes=44 * 1024 * 1024
         ),
     )(
         grads_matrix.reshape(M, S, Q, W),
         grads_vector.reshape(V, W),
         master_matrix, master_vector, moment_matrix, moment_vector, second_matrix, second_vector,
-    )
-    factor = clip[0, 0]
-    master_mat, moment_mat, second_mat = adam_piece(
-        tot.astype(f32), master_matrix, moment_matrix, second_matrix, factor, decay_rate
-    )
-    master_vec, moment_vec, second_vec = adam_piece(
-        vtot[:V], master_vector, moment_vector, second_vector, factor, 0.0
     )
     return (
         master_mat,
@@ -361,7 +354,7 @@
         second_mat,
         second_vec,
         wout.reshape(M, D, W),
-        vecw[:V].astype(bf16),
+        vout,
     )
 
 

time: 131 us -> 115 us (0.88)
  Pallas kernels: 115 us -> 101 us
  other arithmetic: 9.74 us -> 0.01 us
  local copies, waits for them, and re-layouts: 5.29 us -> 12.9 us
    pallas_call x1, Pallas kernels: 115 us -> 101 us  [body(): pl.pallas_call(functools.partial(kernel, R, S, count), out_shape=(mat, ve...]
    unnamed x15 -> x20, local copies, waits for them, and re-layouts: 2.74 us -> 12.9 us
    sub x2 -> x0, other arithmetic: 9.74 us -> none  [adam_piece(): master_next = master - learn_rate * (update + decay * master)]
    slice x2 -> x0, local copies, waits for them, and re-layouts: 2.55 us -> none  [the longest x1 1.36 us: body(): vecw[:V].astype(bf16)]
where the time goes in v2:
time: 115 us; the launch traced here: 114 us
  Pallas kernels  101 us (88%)
  local copies, waits for them, and re-layouts  12.9 us (11%)
    pallas_call x1, Pallas kernels, body(): pl.pallas_call(functools.partial(kernel, R, S, count), out_shape=(mat, ve...  101 us
    unnamed x20, local copies, waits for them, and re-layouts  12.9 us

profile of v2, /device:TPU:1, one launch (start us, length us, event | category | flops | bytes accessed | tf_op | source)
XLA Modules:
  0.0 114.4 jit_solution(18299381314809827758)
XLA Ops:
  0.6 0.0 copy-start
  0.6 0.7 copy-done
  1.4 0.0 copy-start.1
  1.4 0.7 copy-done.1
  2.1 0.0 copy-start.2
  2.1 0.7 copy-done.2
  2.7 0.0 copy-start.3
  2.8 0.7 copy-done.3
  3.4 100.8 %shard_map.143 = (f32[3,256,1024]{2,1,0:T(8,128)S(1)}, f32[5,256]{1,0:T(8,128)S(1)}, f32[3,256,1024]{2,1,0:T(8,128)S(1)}, f32[5,256]{1,0:T(8,128)S(1)}, f32[3,25...) custom-call(bf16[3,4,256,1024]{3,2,1,0:T(8,128)(2,1)} %bitcast.4, ...), custom_call_target="tpu_custom_call" | custom-call | tf_op jit(solution)/shard_map/pallas_call | solution.py:306
  104.2 0.0 slice-start
  104.3 1.7 %copy.24 = f32[3,256,1024]{2,1,0:T(8,128)} copy(f32[3,256,1024]{2,1,0:T(8,128)S(1)} %get-tuple-element.32) | data formatting | bytes 6291456
  105.9 0.6 copy.25
  106.5 0.0 slice-start.1
  106.5 1.7 %copy.26 = f32[3,256,1024]{2,1,0:T(8,128)} copy(f32[3,256,1024]{2,1,0:T(8,128)S(1)} %get-tuple-element.34) | data formatting | bytes 6291456
  108.2 0.6 copy.27
  108.8 1.7 %copy.28 = f32[3,256,1024]{2,1,0:T(8,128)} copy(f32[3,256,1024]{2,1,0:T(8,128)S(1)} %get-tuple-element.36) | data formatting | bytes 6291456
  110.5 0.6 copy.29
  111.1 0.0 slice-done
  111.1 0.0 slice-done.1
  111.1 2.7 %copy.30 = bf16[3,1024,1024]{2,1,0:T(8,128)(2,1)} copy(bf16[3,1024,1024]{2,1,0:T(8,128)(2,1)S(1)} %bitcast.7) | data formatting | bytes 12582912
  113.8 0.6 copy.31
  (1 shorter events, 0.0 us)
Async XLA Ops:
  0.6 0.7 copy-start
  1.4 0.7 copy-start.1
  2.1 0.7 copy-start.2
  2.7 0.7 copy-start.3
  104.2 6.8 %slice-start = ((s8[6291456]{0:T(1024)(128)(4,1)}), s8[4194304]{0:T(1024)(128)(4,1)S(1)}, s32[]{:S(2)}) async-start(s8[6291456]{0:T(1024)(128)(4,1)} %bitcast.5), calls=%async_computation | async-start | bytes 8388608
  106.5 4.5 %slice-start.1 = ((s8[6291456]{0:T(1024)(128)(4,1)}), s8[2097152]{0:T(1024)(128)(4,1)S(1)}, s32[]{:S(2)}) async-start(s8[6291456]{0:T(1024)(128)(4,1)} %bitcast.5), calls=%async_computation.1 | async-start | bytes 4194304

commit v3 on v2

--- a/solution.py
+++ b/solution.py
@@ -35,8 +35,8 @@
     R, S, count,
     gm, gv, mm, mv, om, ov, sm, sv,
     bm, bv, bo, bov, bs, bsv, wout, vout,
-    tot, vecw, acc, rC, rX, rZ, wp, vbuf, rV, sq, sqs, rS, vmine,
-    lsem, csem, xsem, zsem, gsem, vsem, ssem, wzsem, wgsem, wvsem, psem,
+    tot, vecw, acc, rC, rX, rZ, wp, wq, vbuf, rV, sq, sqs, rS, vmine,
+    lsem, csem, xsem, zsem, gsem, vsem, ssem, wzsem, wgsem, wvsem, psem, osem,
 ):
     f32, bf16 = jnp.float32, jnp.bfloat16
     n = int(math.log2(R))
@@ -100,11 +100,11 @@
     vbuf[0, 0:5, :] = gv[...].astype(f32)
     pl.semaphore_wait(barrier, n + S - 1)
 
+    cV = {0: [remote(vbuf.at[0], rV.at[0], vsem.at[0, 0], vsem.at[1, 0], rep=twin)]}
     cC = []
     for k in range(K):
         m, j = k // SPLIT, k % SPLIT
         cC.append(remote(gm.at[m, :, :, otcol(j)], rC.at[k], csem.at[0, k], csem.at[1, k], rep=twin))
-    cV = {0: [remote(vbuf.at[0], rV.at[0], vsem.at[0, 0], vsem.at[1, 0], rep=twin)]}
     ins = []
     for i, (a, b) in enumerate(((mm, bm), (om, bo), (sm, bs))):
         cp = pltpu.make_async_copy(a, b, psem.at[i])
@@ -194,8 +194,8 @@
     for k in range(K):
         first = 8 * (k + 1)
         for st in range(2 * n + 1):
-            order.append((0 if st == 0 else first + 5 * (st - 1), k, st))
-    order += [(12 * t, K, t) for t in range(n + 1)]
+            order.append((0 if st == 0 else first + 8 * (st - 1), k, st))
+    order += [(-1 if t == 0 else 1 if t == 1 else 7 * t, K, t) for t in range(n + 1)]
     for _, k, st in sorted(order):
         if k < K:
             stage(k, st)
@@ -239,6 +239,8 @@
     wV = [remote(vmine, vecw.at[:, mycols], wvsem.at[0, d - 1], wvsem.at[1, d - 1], shard=zpeer[d]) for d in range(1, S)]
     vecw[:, mycols] = vmine[...]
 
+    outs = []
+
     def update(m):
         @pl.loop(0, Q // 16)
         def _(b):
@@ -246,7 +248,11 @@
             one, two, three = adam_piece(
                 tot[m, rows, :].astype(f32), bm[m, rows, :], bo[m, rows, :], bs[m, rows, :], clip, decay_rate)
             bm[m, rows, :], bo[m, rows, :], bs[m, rows, :] = one, two, three
-            wout[m, z, rows, :] = one.astype(bf16)
+            wq[m, rows, :] = one.astype(bf16)
+
+        cp = pltpu.make_async_copy(wq.at[m], wout.at[m, z], osem.at[m])
+        cp.start()
+        outs.append(cp)
 
     units = [(m, d) for m in range(M) for d in range(1, S)]
 
@@ -261,9 +267,9 @@
             part = wout.at[m, zfrom[d], pl.ds(off[i], sizes[i]), myhalf]
             wG[u, i] = remote(part, part, wgsem.at[0, u, i], wgsem.at[1, u, i], rep=partners[i - 1] if i else twin)
 
-    lag = [0, 2, 4, 5] if n == 3 else [2 * i for i in range(n + 1)]
+    lag = [0, 3, 6, 7] if n == 3 else [2 * i for i in range(n + 1)]
     order = [(u + lag[st], -st, u) for u in range(len(units)) for st in range(n + 1)]
-    order += [(2 * m + 1, -n - 1, m) for m in range(M)]
+    order += [(4 * m + 2, -n - 1, m) for m in range(M)]
     for _, st, u in sorted(order):
         if st == -n - 1:
             update(u)
@@ -271,6 +277,8 @@
             spread(u, -st)
     for cp in wV:
         cp.wait_recv()
+    for cp in outs:
+        cp.wait()
     vout[...] = vecw[0:5, :].astype(bf16)
     for cp in sends:
         cp.wait_send()
@@ -311,7 +319,7 @@
             jax.ShapeDtypeStruct((V, W), bf16),
         ),
         in_specs=[hbm, vspec, hbm, vspec, hbm, vspec, hbm, vspec],
-        out_specs=(vspec,) * 8,
+        out_specs=(vspec,) * 6 + (hbm, vspec),
         scratch_shapes=[
             pltpu.VMEM((M, Q, W), bf16),
             pltpu.VMEM((8, W), f32),
@@ -320,6 +328,7 @@
             [pltpu.VMEM((K, S, Q >> (i + 1), cw), bf16) for i in range(n - 1)],
             pltpu.VMEM((K, S - 1, pr, cw), bf16),
             pltpu.VMEM((M, pr, half), bf16),
+            pltpu.VMEM((M, Q, W), bf16),
             pltpu.VMEM((n + 2, 8, W), f32),
             pltpu.VMEM((n + S - 1, 8, W), f32),
             pltpu.VMEM((8, cw), f32),
@@ -337,6 +346,7 @@
             dma((2, U, n)),
             dma((2, S - 1)),
             dma((3,)),
+            dma((M,)),
         ],
         compiler_params=pltpu.CompilerParams(
             collective_id=0, has_side_effects=True, vmem_limit_bytes=44 * 1024 * 1024

time: 115 us -> 107 us (0.930)
  Pallas kernels: 101 us -> 93.5 us
    pallas_call x1, Pallas kernels: 101 us -> 93.5 us  [body(): pl.pallas_call(functools.partial(kernel, R, S, count), out_shape=(mat, ve...]
where the time goes in v3:
time: 107 us
  Pallas kernels  93.5 us (87%)
  local copies, waits for them, and re-layouts  12.9 us (12%)
    pallas_call x1, Pallas kernels, body(): pl.pallas_call(functools.partial(kernel, R, S, count), out_shape=(mat, ve...  93.5 us
    unnamed x20, local copies, waits for them, and re-layouts  12.9 us

profile of v3, /device:TPU:1, one launch (start us, length us, event | category | flops | bytes accessed | tf_op | source)
XLA Modules:
  0.0 107.1 jit_solution(16851835537151988975)
XLA Ops:
  0.6 0.0 copy-start
  0.6 0.7 copy-done
  1.4 0.0 copy-start.1
  1.4 0.7 copy-done.1
  2.1 0.0 copy-start.2
  2.1 0.7 copy-done.2
  2.7 0.0 copy-start.3
  2.8 0.7 copy-done.3
  3.4 93.5 %shard_map.143 = (f32[3,256,1024]{2,1,0:T(8,128)S(1)}, f32[5,256]{1,0:T(8,128)S(1)}, f32[3,256,1024]{2,1,0:T(8,128)S(1)}, f32[5,256]{1,0:T(8,128)S(1)}, f32[3,25...) custom-call(bf16[3,4,256,1024]{3,2,1,0:T(8,128)(2,1)} %bitcast.4, ...), custom_call_target="tpu_custom_call" | custom-call | tf_op jit(solution)/shard_map/pallas_call | solution.py:314
  96.9 0.0 slice-start
  97.0 1.7 %copy.24 = f32[3,256,1024]{2,1,0:T(8,128)} copy(f32[3,256,1024]{2,1,0:T(8,128)S(1)} %get-tuple-element.32) | data formatting | bytes 6291456
  98.6 0.6 copy.25
  99.2 0.0 slice-start.1
  99.2 1.7 %copy.26 = f32[3,256,1024]{2,1,0:T(8,128)} copy(f32[3,256,1024]{2,1,0:T(8,128)S(1)} %get-tuple-element.34) | data formatting | bytes 6291456
  100.9 0.6 copy.27
  101.5 1.7 %copy.28 = f32[3,256,1024]{2,1,0:T(8,128)} copy(f32[3,256,1024]{2,1,0:T(8,128)S(1)} %get-tuple-element.36) | data formatting | bytes 6291456
  103.2 0.6 copy.29
  103.8 0.0 slice-done
  103.8 0.0 slice-done.1
  103.8 2.7 %copy.30 = bf16[3,1024,1024]{2,1,0:T(8,128)(2,1)} copy(bf16[3,1024,1024]{2,1,0:T(8,128)(2,1)S(1)} %bitcast.7) | data formatting | bytes 12582912
  106.5 0.6 copy.31
  (1 shorter events, 0.0 us)
Async XLA Ops:
  0.6 0.7 copy-start
  1.4 0.7 copy-start.1
  2.1 0.7 copy-start.2
  2.7 0.7 copy-start.3
  96.9 6.8 %slice-start = ((s8[6291456]{0:T(1024)(128)(4,1)}), s8[4194304]{0:T(1024)(128)(4,1)S(1)}, s32[]{:S(2)}) async-start(s8[6291456]{0:T(1024)(128)(4,1)} %bitcast.5), calls=%async_computation | async-start | bytes 8388608
  99.2 4.5 %slice-start.1 = ((s8[6291456]{0:T(1024)(128)(4,1)}), s8[2097152]{0:T(1024)(128)(4,1)S(1)}, s32[]{:S(2)}) async-start(s8[6291456]{0:T(1024)(128)(4,1)} %bitcast.5), calls=%async_computation.1 | async-start | bytes 4194304
